TPU v7x, 512 devices: a whole 4x8x8 slice. The times are simulated.
512 devices in a mesh: row: 16 (over z, x_lo), col: 32 (over y, x_hi, core).
Axes of the slice: x: 4 (x_hi: 2, x_lo: 2; x = x_hi * 2 + x_lo), y: 8, z: 8, core: 2. Of those that a mesh axis runs over, the one named last changes fastest.
Arguments:
- weights: bfloat16 [8192, 8192], P('row', 'col'), may hold values from -32 to 32, as said below
Outputs:
- edge_cycles: float32 [8192, 8192], P('row', 'col')
- account_cycles: float32 [8192], P(('row', 'col'))
Inputs may be any that keep to these rules, and one draw needn't show every extreme that they name: `weights`: about half of the entries are zero.
All inputs are finite; a program needn't handle non-finite values.
Results may differ from a plain program's by a relative error of at most 0.0003.
Values may be sent and summed in bfloat16 or wider, within the bound.
A program may use at most 64 MiB of HBM per device.

v0:
```python
import math

import jax
import jax.numpy as jnp
from jax import lax
from jax.sharding import PartitionSpec as P


def body(weights):
    row_block = weights.shape[0]
    col_block = weights.shape[1]
    row_panel = lax.all_gather(weights, "col", axis=1, tiled=True)
    accounts = row_panel.shape[1]
    my_col = lax.axis_index("col")
    row_count = lax.axis_size("row")
    col_count = lax.axis_size("col")
    paths = jnp.dot(
        row_panel,
        lax.all_gather(weights, "row", axis=0, tiled=True),
        preferred_element_type=jnp.float32,
    )
    spread = lax.all_to_all(
        lax.all_to_all(weights, "row", split_axis=1, concat_axis=0, tiled=True),
        "col",
        split_axis=0,
        concat_axis=1,
        tiled=True,
    )
    settled = lax.all_to_all(spread, "row", split_axis=1, concat_axis=0, tiled=True)
    groups = col_count // row_count
    width = col_block // row_count
    pieces = settled.reshape(row_count, col_block, groups, width)
    tile = jnp.transpose(pieces, (1, 2, 0, 3)).reshape(col_block, row_block)
    mirror_tile = tile.T
    edge_cycles = paths * mirror_tile.astype(jnp.float32) * (2.0 / math.sqrt(accounts))
    partial_value = jnp.sum(edge_cycles, axis=1)
    summed = lax.psum(partial_value, "col")
    share = row_block // col_count
    account_cycles = lax.dynamic_slice_in_dim(summed, my_col * share, share, 0)
    account_cycles = account_cycles / math.sqrt(accounts)
    return (edge_cycles, account_cycles)


def solution(mesh):
    return jax.shard_map(
        body,
        mesh=mesh,
        in_specs=(P("row", "col"),),
        out_specs=(P("row", "col"), P(("row", "col"))),
        check_vma=False,
    )
```

profile of v0, /device:TPU:1, one launch (start us, length us, event | category | flops | bytes accessed | tf_op | source)
XLA Modules:
  0.0 322.0 jit_solution(15294834991217454340)
XLA Ops:
  7.2 0.0 all-gather.5.cloned.1.call-start
  7.2 0.7 all-gather.5.cloned.1.call-update
  7.9 0.0 all-gather.3.cloned.1.call-start
  7.9 0.7 all-gather.3.cloned.1.call-update
  8.6 1.1 copy.10
  9.7 22.2 %all_to_all.48 = bf16[512,16,16]{0,2,1:T(8,128)(2,1)S(1)} all-to-all(bf16[512,16,16]{0,2,1:T(8,128)(2,1)S(1)} %bitcast.20), channel_id=1, replica_groups=mesh['row'=16,'col'=32] {'row'}, dimensions={1} | all-to-all | bytes 524288 | tf_op jit(solution)/shard_map/all_to_all | solution.py:23
  31.9 0.1 copy.11
  32.1 0.1 all_to_all.39
  32.2 0.2 copy.12
  32.3 24.8 %all_to_all.49 = bf16[32,256,16]{1,2,0:T(8,128)(2,1)} all-to-all(bf16[32,256,16]{1,2,0:T(8,128)(2,1)S(1)} %copy.12), channel_id=1, replica_groups=mesh['row'=16,'col'=32] {'col'}, dimensions={0} | all-to-all | bytes 524288 | tf_op jit(solution)/shard_map/all_to_all | solution.py:22
  57.1 3.5 %all-to-all-start.2 = ((bf16[256,16,32]{0,2,1:T(8,128)(2,1)}), bf16[256,16,32]{0,2,1:T(8,128)(2,1)S(1)}, u32[]{:S(2)}, u32[]{:S(2)}) async-start(bf16[256,16,32]{0,2,1:T(8,128)(2,1)} %bitcast.3), calls=%async_computation.2 | async-start | bytes 524288 | tf_op jit(solution)/shard_map/all_to_all | solution.py:29
  60.7 15.0 %all-to-all-done.2 = bf16[256,16,32]{0,2,1:T(8,128)(2,1)S(1)} async-done(((bf16[256,16,32]{0,2,1:T(8,128)(2,1)}), bf16[256,16,32]{0,2,1:T(8,128)(2,1)S(1)}, u32[]{:S(2)}, u32[]{:S(2)}) %all-to-all-start.2) | async-done | bytes 262176 | tf_op jit(solution)/shard_map/all_to_all | solution.py:29
  75.8 0.2 copy.14
  76.0 46.4 %all-gather.5.cloned.1.call-done = bf16[8192,256]{1,0:T(8,128)(2,1)} async-done(((bf16[512,256]{1,0:T(8,128)(2,1)}), bf16[8192,256]{1,0:T(8,128)(2,1)}) %all-gather.5.cloned.1.call-update) | async-done | bytes 4194320 | tf_op jit(solution)/shard_map/all_gather | solution.py:19
  122.3 119.7 %all-gather.3.cloned.1.call-done = bf16[512,8192]{1,0:T(8,128)(2,1)} async-done(((bf16[512,256]{1,0:T(8,128)(2,1)}), bf16[512,8192]{1,0:T(8,128)(2,1)}) %all-gather.3.cloned.1.call-update) | async-done | bytes 8388624 | tf_op jit(solution)/shard_map/all_gather | solution.py:12
  242.0 7.0 %fusion.1 = (f32[512]{0:T(512)S(1)}, f32[512,256]{0,1:T(8,128)S(1)}) fusion(f32[256,512]{1,0:T(8,128)S(1)} %copy.14, bf16[512,8192]{1,0:T(8,128)(2,1)} %all-gather.3.cloned.1.call-done, bf16[8192,256]{1,0:T(8,128)(2,1)} %all-gather.5.cloned.1.call-done), kind=kOutput, calls=%fused_computation.3 | convolution fusion | flops 2147876352 | bytes 13633536 | tf_op jit(solution)/shard_map/dot_general | solution.py:17
  249.0 1.0 copy.15
  250.0 64.6 %psum.7 = f32[512]{0:T(512)S(1)} all-reduce(f32[512]{0:T(512)S(1)} %get-tuple-element.8), channel_id=1, replica_groups=mesh['row'=16,'col'=32] {'col'}, use_global_device_ids=true, to_apply=%region_1.0 | all-reduce | flops 512 | bytes 4096 | tf_op jit(solution)/shard_map/psum | solution.py:37
  314.6 0.6 dynamic-slice_multiply_fusion
  (2 shorter events, 0.1 us)
Async XLA Ops:
  7.2 115.2 %all-gather.5.cloned.1.call-start = ((), (), s32[]{:S(2)}) async-start(), calls=%async_computation.4 | async-start | bytes 4456448 | tf_op jit(solution)/shard_map/all_gather | solution.py:19
  7.9 234.1 %all-gather.3.cloned.1.call-start = ((), (), s32[]{:S(2)}) async-start(), calls=%async_computation.3 | async-start | bytes 8650752 | tf_op jit(solution)/shard_map/all_gather | solution.py:12
  57.1 18.6 %all-to-all-start.2 = ((bf16[256,16,32]{0,2,1:T(8,128)(2,1)}), bf16[256,16,32]{0,2,1:T(8,128)(2,1)S(1)}, u32[]{:S(2)}, u32[]{:S(2)}) async-start(bf16[256,16,32]{0,2,1:T(8,128)(2,1)} %bitcast.3), calls=%async_computation.2 | async-start | bytes 524288 | tf_op jit(solution)/shard_map/all_to_all | solution.py:29
Sparse Core Ops, SparseCore 0:
  10.1 112.2 all-gather.4
  125.5 116.4 all-gather.2
where the time goes:
time: 324 us; the launch traced here: 322 us
  waiting for transfers between devices  182 us (56%)
  blocking collectives  112 us (35%)
  between operations  14.1 us (4%)
  matrix products  6.96 us (2%)
  starting transfers between devices  3.61 us (1%)
    all_gather x1, waiting for transfers between devices, body(): row_panel = lax.all_gather(weights, 'col', axis=1, tiled=True)  120 us
    psum x1, blocking collectives, body(): summed = lax.psum(partial_value, 'col')  64.6 us
    all_gather x1, waiting for transfers between devices, body(): lax.all_gather(weights, 'row', axis=0, tiled=True)  46.4 us
    all_to_all x1, blocking collectives, body(): lax.all_to_all(lax.all_to_all(weights, 'row', split_axis=1, concat_axis=0...  24.8 us
    all_to_all x1, blocking collectives, body(): lax.all_to_all(weights, 'row', split_axis=1, concat_axis=0, tiled=True)  22.2 us
    all_to_all x1, waiting for transfers between devices, body(): lax.all_to_all(spread, 'row', split_axis=1, concat_axis=0, tiled=True)  15 us
    dot_general x1, matrix products, body(): jnp.dot(row_panel, lax.all_gather(weights, 'row', axis=0, tiled=True), pr...  6.96 us
  transfers between devices with their start and end apart: 3, of which 3 were waited for; matrix products, arithmetic and copies ran while one was open for 1% of the time, Pallas kernels for 0%

commit v1 on v0

v1 whole, which is shorter than its diff:
```python
import math

import jax
import jax.numpy as jnp
from jax import lax
from jax.experimental import pallas as pl
from jax.experimental.pallas import tpu as pltpu
from jax.sharding import PartitionSpec as P

MESH = pl.DeviceIdType.MESH
PHASES = 4


def kernel(
    w_ref, edge_ref, acct_ref,
    a_buf, b_buf, part, inbox, tbuf, sums_out, sums_in,
    ra_send, ra_recv, rb_send, rb_recv,
    y_send, y_recv, z_send, z_recv, d_send, d_recv,
    c_send, c_recv, t_send, t_recv, s_send, s_recv,
):
    row, col = lax.axis_index("row"), lax.axis_index("col")
    z, s = row // 2, row % 2
    y, h, c = col // 4, (col // 2) % 2, col % 2
    x = 2 * h + s
    accounts = 8192

    def dev(y_, z_, x_, c_):
        return (2 * z_ + x_ % 2, 4 * y_ + 2 * (x_ // 2) + c_)

    def up(v, d, n):
        return lax.rem(v + (d + n), n)

    def remote(src, dst, send, recv, target):
        return pltpu.make_async_remote_copy(
            src_ref=src, dst_ref=dst, send_sem=send, recv_sem=recv,
            device_id=target, device_id_type=MESH,
        )

    barrier = pltpu.get_barrier_semaphore()
    senders = [
        dev(up(y, 1, 8), z, x, c), dev(up(y, -1, 8), z, x, c),
        dev(y, up(z, 1, 8), x, c), dev(y, up(z, -1, 8), x, c),
        dev(y, z, up(x, 1, 4), c), dev(y, z, up(x, -1, 4), c),
        dev(y, z, x, 1 - c),
        dev(y, z, 2 * h + c, s),
        dev(y, z, h, c), dev(y, z, 2 + h, c),
    ]
    for m in range(8):
        for k in range(2):
            senders.append(dev(z, m, 2 * h + c, k))
            senders.append(dev(z, m, 2 * s + k, y // 4))
    for target in senders:
        pl.semaphore_signal(barrier, inc=1, device_id=target, device_id_type=MESH)
    pl.semaphore_wait(barrier, len(senders))

    a_self = s == c
    a_target = dev(y, z, 2 * h + c, s)

    def lanes(v):
        return pl.ds(pl.multiple_of(v * 256, 256), 256)

    def move_a(p):
        return remote(
            w_ref.at[pl.ds(128 * p, 128), :], a_buf.at[s, p, :, lanes(y)],
            ra_send.at[p], ra_recv.at[p], a_target,
        )

    def move_a_local(p):
        return pltpu.make_async_copy(
            w_ref.at[pl.ds(128 * p, 128), :], a_buf.at[s, p, :, lanes(y)], ra_recv.at[p]
        )

    def arrived_a(p):
        return remote(
            a_buf.at[c, p, :, lanes(y)], a_buf.at[c, p, :, lanes(y)],
            ra_send.at[p], ra_recv.at[p], a_target,
        )

    def rows(v):
        return pl.ds(pl.multiple_of(v * 256, 256), 256)

    def move_b(half, j):
        return remote(
            w_ref.at[pl.ds(256 * half, 256), pl.ds(128 * j, 128)], b_buf.at[h, j, rows(z), :],
            rb_send.at[half, j], rb_recv.at[h, j], dev(y, z, 2 * s + half, c),
        )

    def move_b_local(half, j):
        return pltpu.make_async_copy(
            w_ref.at[pl.ds(256 * half, 256), pl.ds(128 * j, 128)], b_buf.at[h, j, rows(z), :],
            rb_recv.at[h, j],
        )

    def arrived_b(p):
        hh, j = (p + c) % 2, p // 2
        return remote(
            b_buf.at[hh, j, rows(z), :], b_buf.at[hh, j, rows(z), :],
            rb_send.at[0, 0], rb_recv.at[hh, j], a_target,
        )

    for p in range(PHASES):
        @pl.when(a_self)
        def _():
            move_a_local(p).start()

        @pl.when(jnp.logical_not(a_self))
        def _():
            move_a(p).start()

        @pl.when((p + c) % 2 == h)
        def _():
            for half in range(2):
                @pl.when(x == 2 * s + half)
                def _():
                    move_b_local(half, p // 2).start()

                @pl.when(x != 2 * s + half)
                def _():
                    move_b(half, p // 2).start()

    right = (4, 3, 4, 3)

    def hop_a(p, direction, k):
        yy = up(y, -direction * k, 8)
        block = a_buf.at[c, p, :, lanes(yy)]
        return remote(
            block, block, y_send.at[p, (1 - direction) // 2, k], y_recv.at[p, yy],
            dev(up(y, direction, 8), z, x, c),
        )

    def hop_b(p, direction, k):
        zz = up(z, -direction * k, 8)
        block = b_buf.at[(p + c) % 2, p // 2, rows(zz), :]
        return remote(
            block, block, z_send.at[p, (1 - direction) // 2, k], z_recv.at[p, zz],
            dev(y, up(z, direction, 8), x, c),
        )

    def share(p, yy, owner=None):
        block = a_buf.at[c if owner is None else owner, p, :, lanes(yy)]
        return remote(block, block, d_send.at[p, yy], d_recv.at[p, yy], dev(y, z, x, 1 - c))

    def steps(p, direction):
        return right[p] if direction == 1 else 7 - right[p]

    def place(i, p):
        return (p + c) % 2, p // 2, 1 - 2 * ((i + p // 2) % 2)

    def product(i, p):
        hh, j, _ = place(i, p)
        left = a_buf[:, i].reshape(256, 2048)
        value = jnp.dot(left, b_buf[hh, j], preferred_element_type=jnp.float32)
        part[0, hh, i, j] = value[:128]
        part[1, hh, i, j] = value[128:]

    def roles(i, p, k):
        hh, j, way = place(i, p)
        delta = lax.rem(2 * hh + k + 4 - x, 4)
        relay = lax.rem(way + 4, 4)
        far = delta == 2
        passes = delta == relay
        direct = jnp.logical_and(delta % 2 == 1, jnp.logical_not(passes))
        step = jnp.where(far, way, 2 - delta)
        kind = jnp.where(far, 0, (delta + 1) // 2)
        copy = remote(
            part.at[k, hh, i, j], inbox.at[kind, i, j], c_send.at[k, hh, i, j], c_recv.at[kind, i, j],
            dev(y, z, lax.rem(x + step + 4, 4), c),
        )
        return far, passes, direct, copy

    def landed(kind, i, j):
        return remote(
            inbox.at[kind, i, j], inbox.at[kind, i, j], c_send.at[0, 0, i, j], c_recv.at[kind, i, j],
            a_target,
        )

    def tiles(q):
        return [(q, p) for p in range(q + 1)], [(i, q) for i in range(q)]

    def each(q, action):
        @pl.loop(0, q + 1)
        def _(p):
            action(q, p)

        if q:
            @pl.loop(0, q)
            def _(i):
                action(i, q)

    def first(i, p):
        product(i, p)
        for k in range(2):
            far, _, direct, copy = roles(i, p, k)

            @pl.when(jnp.logical_or(far, direct))
            def _():
                copy.start()

    def second(i, p):
        hh, j, _ = place(i, p)
        for k in range(2):
            _, passes, _, copy = roles(i, p, k)

            @pl.when(passes)
            def _():
                landed(0, i, j).wait_recv()
                part[k, hh, i, j] += inbox[0, i, j]
                copy.start()

    def mirror(u, hh):
        src = b_buf.at[hh, :, pl.ds(pl.multiple_of(u * 256 + z * 32, 32), 32), :]
        dst = tbuf.at[c, :, pl.ds(pl.multiple_of(z * 32, 32), 32), :]
        own = (u == y) & (hh == s) & (s == c) & (y == z)
        copy = remote(src, dst, t_send.at[u, hh], t_recv.at[c, z], dev(u, y, 2 * h + hh, s))
        local = pltpu.make_async_copy(src, dst, t_recv.at[c, z])
        return own, copy, local

    for slot in range(2 * PHASES + 3):
        for p in range(PHASES):
            k = slot - 2 * p
            if k == 0:
                arrived_a(p).wait_recv()
                for direction in (1, -1):
                    hop_a(p, direction, 0).start()
                arrived_b(p).wait_recv()
                for direction in (1, -1):
                    hop_b(p, direction, 0).start()
                share(p, y).start()
            elif 1 <= k <= 4:
                for direction in (1, -1):
                    if k <= steps(p, direction):
                        hop_a(p, direction, k).wait_recv()
                        if k < steps(p, direction):
                            hop_a(p, direction, k).start()
                        share(p, up(y, -direction * k, 8)).start()
                    if k <= steps(p, direction):
                        hop_b(p, direction, k).wait_recv()
                        if k < steps(p, direction):
                            hop_b(p, direction, k).start()
        if slot == 2 * PHASES + 2:
            @pl.loop(0, 8)
            def _(u):
                for hh in range(2):
                    own, copy, local = mirror(u, hh)

                    @pl.when(own)
                    def _():
                        local.start()

                    @pl.when(jnp.logical_not(own))
                    def _():
                        copy.start()

        for p in range(PHASES):
            k = slot - 2 * p
            if k == 4:
                for yy in range(8):
                    share(p, yy, 1 - c).wait_recv()
                each(p, first)
            elif k == 5 and p < PHASES - 1:
                each(p, second)
    each(PHASES - 1, second)

    for k in range(2):
        for m in range(8):
            dst = tbuf.at[k, :, pl.ds(32 * m, 32), :]
            remote(dst, dst, t_send.at[0, 0], t_recv.at[k, m], a_target).wait_recv()
    scale = 2.0 / math.sqrt(accounts)
    for j in range(2):
        sums_out[j] = jnp.zeros((1, 128), jnp.float32)
        for i in range(4):
            landed(1, i, j).wait_recv()
            landed(2, i, j).wait_recv()
            paths = part[s, h, i, j] + inbox[1, i, j] + inbox[2, i, j]
            back = tbuf[i // 2, i % 2, pl.ds(128 * j, 128), :].astype(jnp.float32).T
            value = paths * back * scale
            edge_ref[pl.ds(128 * i, 128), pl.ds(128 * j, 128)] = value
            sums_out[j] += jnp.sum(value, axis=0, keepdims=True)

    def deliver(t):
        cc = 16 * c + t
        own = (y == z) & (h == s) & (cc == col)
        copy = remote(
            sums_out.at[t // 8], sums_in.at[row], s_send.at[t], s_recv.at[row], (2 * y + h, cc)
        )
        local = pltpu.make_async_copy(sums_out.at[t // 8], sums_in.at[row], s_recv.at[row])
        return own, copy, local

    for t in range(16):
        own, copy, local = deliver(t)

        @pl.when(own)
        def _():
            local.start()

        @pl.when(jnp.logical_not(own))
        def _():
            copy.start()

    for p in range(PHASES):
        @pl.when(jnp.logical_not(a_self))
        def _():
            move_a(p).wait_send()

        @pl.when((p + c) % 2 == h)
        def _():
            for half in range(2):
                @pl.when(x != 2 * s + half)
                def _():
                    move_b(half, p // 2).wait_send()

        for direction in (1, -1):
            for k in range(steps(p, direction)):
                hop_a(p, direction, k).wait_send()
                hop_b(p, direction, k).wait_send()
        for yy in range(8):
            share(p, yy).wait_send()

        @pl.loop(0, PHASES)
        def _(i):
            for k in range(2):
                far, passes, direct, copy = roles(i, p, k)

                @pl.when(far | passes | direct)
                def _():
                    copy.wait_send()

    @pl.loop(0, 8)
    def _(u):
        for hh in range(2):
            own, copy, _ = mirror(u, hh)

            @pl.when(jnp.logical_not(own))
            def _():
                copy.wait_send()

    total = jnp.zeros((1, 128), jnp.float32)
    for r in range(16):
        remote(sums_in.at[r], sums_in.at[r], s_send.at[r], s_recv.at[r], a_target).wait_recv()
        total = total + sums_in[r]
    total = total * (1.0 / math.sqrt(accounts))
    share_of = pltpu.roll(total, lax.rem(128 - 16 * (col % 8), 128), 1)
    acct_ref[...] = share_of[:, :16]
    for t in range(16):
        own, copy, _ = deliver(t)

        @pl.when(jnp.logical_not(own))
        def _():
            copy.wait_send()


def body(weights):
    dma = pltpu.SemaphoreType.DMA
    edge, acct = pl.pallas_call(
        kernel,
        out_shape=(
            jax.ShapeDtypeStruct((512, 256), jnp.float32),
            jax.ShapeDtypeStruct((1, 16), jnp.float32),
        ),
        in_specs=[pl.BlockSpec(memory_space=pltpu.VMEM)],
        out_specs=(
            pl.BlockSpec(memory_space=pltpu.VMEM),
            pl.BlockSpec(memory_space=pltpu.VMEM),
        ),
        scratch_shapes=[
            pltpu.VMEM((2, 4, 128, 2048), jnp.bfloat16),
            pltpu.VMEM((2, 2, 2048, 128), jnp.bfloat16),
            pltpu.VMEM((2, 2, 4, 2, 128, 128), jnp.float32),
            pltpu.VMEM((3, 4, 2, 128, 128), jnp.float32),
            pltpu.VMEM((2, 2, 256, 128), jnp.bfloat16),
            pltpu.VMEM((2, 1, 128), jnp.float32),
            pltpu.VMEM((16, 1, 128), jnp.float32),
            dma((4,)), dma((4,)), dma((2, 2)), dma((2, 2)),
            dma((4, 2, 4)), dma((4, 8)), dma((4, 2, 4)), dma((4, 8)), dma((4, 8)), dma((4, 8)),
            dma((2, 2, 4, 2)), dma((3, 4, 2)), dma((8, 2)), dma((2, 8)), dma((16,)), dma((16,)),
        ],
        compiler_params=pltpu.CompilerParams(
            collective_id=0, has_side_effects=True, vmem_limit_bytes=32 * 1024 * 1024
        ),
        name="cycles",
    )(weights)
    return edge, acct.reshape(16)


def solution(mesh):
    return jax.shard_map(
        body,
        mesh=mesh,
        in_specs=(P("row", "col"),),
        out_specs=(P("row", "col"), P(("row", "col"))),
        check_vma=False,
    )
```

time: 324 us -> 90.2 us (0.28)
  the two profiles are of different devices: /device:TPU:1 before, /device:TPU:2 now
where the time goes in v1:
time: 90.2 us; the launch traced here: 90.1 us
  Pallas kernels  87.2 us (97%)
  local copies, waits for them, and re-layouts  2.25 us (2%)
    pallas_call x1, Pallas kernels, body(): pl.pallas_call(kernel, out_shape=(jax.ShapeDtypeStruct((512, 256), jnp.fl...  87.2 us
    unnamed x4, local copies, waits for them, and re-layouts  2.25 us

profile of v1, /device:TPU:2, one launch (start us, length us, event | category | flops | bytes accessed | tf_op | source)
XLA Modules:
  0.0 90.1 jit_solution(12719249004913826315)
XLA Ops:
  0.6 0.0 copy-start
  0.6 0.9 %copy-done = bf16[512,256]{1,0:T(8,128)(2,1)S(1)} copy-done((bf16[512,256]{1,0:T(8,128)(2,1)S(1)}, bf16[512,256]{1,0:T(8,128)(2,1)}, u32[]{:S(2)}) %copy-start) | copy-done | bytes 262168
  1.6 87.2 %cycles.1 = (f32[512,256]{1,0:T(8,128)S(1)}, f32[1,16]{1,0:T(1,128)S(1)}) custom-call(bf16[512,256]{1,0:T(8,128)(2,1)S(1)} %copy-done), custom_call_target="tpu_custom_call" | custom-call | tf_op jit(solution)/shard_map/cycles/pallas_call | solution.py:354
  88.8 0.8 copy.5
  89.6 0.5 copy.6
Async XLA Ops:
  0.6 1.0 %copy-start = (bf16[512,256]{1,0:T(8,128)(2,1)S(1)}, bf16[512,256]{1,0:T(8,128)(2,1)}, u32[]{:S(2)}) copy-start(bf16[512,256]{1,0:T(8,128)(2,1)} %w_ref.1) | copy-start | bytes 786436

commit v2 on v1

--- a/solution.py
+++ b/solution.py
@@ -9,6 +9,7 @@
 
 MESH = pl.DeviceIdType.MESH
 PHASES = 4
+START = (0, 0, 0, 0)
 
 
 def kernel(
@@ -45,9 +46,10 @@
         dev(y, z, 2 * h + c, s),
         dev(y, z, h, c), dev(y, z, 2 + h, c),
     ]
-    for m in range(8):
-        for k in range(2):
-            senders.append(dev(z, m, 2 * h + c, k))
+    for k in range(2):
+        for q in range(2):
+            senders.append(dev(z, (y + z) % 4 + 4 * q, 2 * h + c, k))
+        for m in range(8):
             senders.append(dev(z, m, 2 * s + k, y // 4))
     for target in senders:
         pl.semaphore_signal(barrier, inc=1, device_id=target, device_id_type=MESH)
@@ -62,7 +64,7 @@
     def move_a(p):
         return remote(
             w_ref.at[pl.ds(128 * p, 128), :], a_buf.at[s, p, :, lanes(y)],
-            ra_send.at[p], ra_recv.at[p], a_target,
+            ra_send, ra_recv.at[p], a_target,
         )
 
     def move_a_local(p):
@@ -73,7 +75,7 @@
     def arrived_a(p):
         return remote(
             a_buf.at[c, p, :, lanes(y)], a_buf.at[c, p, :, lanes(y)],
-            ra_send.at[p], ra_recv.at[p], a_target,
+            ra_send, ra_recv.at[p], a_target,
         )
 
     def rows(v):
@@ -82,7 +84,7 @@
     def move_b(half, j):
         return remote(
             w_ref.at[pl.ds(256 * half, 256), pl.ds(128 * j, 128)], b_buf.at[h, j, rows(z), :],
-            rb_send.at[half, j], rb_recv.at[h, j], dev(y, z, 2 * s + half, c),
+            rb_send.at[half], rb_recv.at[h, j], dev(y, z, 2 * s + half, c),
         )
 
     def move_b_local(half, j):
@@ -95,7 +97,7 @@
         hh, j = (p + c) % 2, p // 2
         return remote(
             b_buf.at[hh, j, rows(z), :], b_buf.at[hh, j, rows(z), :],
-            rb_send.at[0, 0], rb_recv.at[hh, j], a_target,
+            rb_send.at[0], rb_recv.at[hh, j], a_target,
         )
 
     for p in range(PHASES):
@@ -124,7 +126,7 @@
         yy = up(y, -direction * k, 8)
         block = a_buf.at[c, p, :, lanes(yy)]
         return remote(
-            block, block, y_send.at[p, (1 - direction) // 2, k], y_recv.at[p, yy],
+            block, block, y_send, y_recv.at[p, yy],
             dev(up(y, direction, 8), z, x, c),
         )
 
@@ -132,13 +134,17 @@
         zz = up(z, -direction * k, 8)
         block = b_buf.at[(p + c) % 2, p // 2, rows(zz), :]
         return remote(
-            block, block, z_send.at[p, (1 - direction) // 2, k], z_recv.at[p, zz],
+            block, block, z_send, z_recv.at[p, zz],
             dev(y, up(z, direction, 8), x, c),
         )
 
-    def share(p, yy, owner=None):
-        block = a_buf.at[c if owner is None else owner, p, :, lanes(yy)]
-        return remote(block, block, d_send.at[p, yy], d_recv.at[p, yy], dev(y, z, x, 1 - c))
+    def share(p, yy):
+        block = a_buf.at[c, p, :, lanes(yy)]
+        return remote(block, block, d_send, d_recv.at[p], dev(y, z, x, 1 - c))
+
+    def shared(p):
+        block = a_buf.at[1 - c, p]
+        return remote(block, block, d_send, d_recv.at[p], a_target)
 
     def steps(p, direction):
         return right[p] if direction == 1 else 7 - right[p]
@@ -163,14 +169,14 @@
         step = jnp.where(far, way, 2 - delta)
         kind = jnp.where(far, 0, (delta + 1) // 2)
         copy = remote(
-            part.at[k, hh, i, j], inbox.at[kind, i, j], c_send.at[k, hh, i, j], c_recv.at[kind, i, j],
+            part.at[k, hh, i, j], inbox.at[kind, i, j], c_send, c_recv.at[kind, i, j],
             dev(y, z, lax.rem(x + step + 4, 4), c),
         )
         return far, passes, direct, copy
 
     def landed(kind, i, j):
         return remote(
-            inbox.at[kind, i, j], inbox.at[kind, i, j], c_send.at[0, 0, i, j], c_recv.at[kind, i, j],
+            inbox.at[kind, i, j], inbox.at[kind, i, j], c_send, c_recv.at[kind, i, j],
             a_target,
         )
 
@@ -207,17 +213,20 @@
                 part[k, hh, i, j] += inbox[0, i, j]
                 copy.start()
 
-    def mirror(u, hh):
-        src = b_buf.at[hh, :, pl.ds(pl.multiple_of(u * 256 + z * 32, 32), 32), :]
-        dst = tbuf.at[c, :, pl.ds(pl.multiple_of(z * 32, 32), 32), :]
+    def mirror(q, hh):
+        u = (z + 8 - y) % 4 + 4 * q
+        half = z // 4
+        src = b_buf.at[hh, :, pl.ds(pl.multiple_of(u * 256 + half * 128, 128), 128), :]
+        dst = tbuf.at[c, :, pl.ds(pl.multiple_of(half * 128, 128), 128), :]
         own = (u == y) & (hh == s) & (s == c) & (y == z)
-        copy = remote(src, dst, t_send.at[u, hh], t_recv.at[c, z], dev(u, y, 2 * h + hh, s))
-        local = pltpu.make_async_copy(src, dst, t_recv.at[c, z])
+        copy = remote(src, dst, t_send.at[q, hh], t_recv, dev(u, y, 2 * h + hh, s))
+        local = pltpu.make_async_copy(src, dst, t_recv)
         return own, copy, local
 
-    for slot in range(2 * PHASES + 3):
+    last = max(START) + 4
+    for slot in range(last + 1):
         for p in range(PHASES):
-            k = slot - 2 * p
+            k = slot - START[p]
             if k == 0:
                 arrived_a(p).wait_recv()
                 for direction in (1, -1):
@@ -237,11 +246,10 @@
                         hop_b(p, direction, k).wait_recv()
                         if k < steps(p, direction):
                             hop_b(p, direction, k).start()
-        if slot == 2 * PHASES + 2:
-            @pl.loop(0, 8)
-            def _(u):
+        if slot == last:
+            for q in range(2):
                 for hh in range(2):
-                    own, copy, local = mirror(u, hh)
+                    own, copy, local = mirror(q, hh)
 
                     @pl.when(own)
                     def _():
@@ -252,101 +260,84 @@
                         copy.start()
 
         for p in range(PHASES):
-            k = slot - 2 * p
+            k = slot - START[p]
             if k == 4:
-                for yy in range(8):
-                    share(p, yy, 1 - c).wait_recv()
+                shared(p).wait_recv()
                 each(p, first)
-            elif k == 5 and p < PHASES - 1:
+            elif k == 5:
                 each(p, second)
-    each(PHASES - 1, second)
-
-    for k in range(2):
-        for m in range(8):
-            dst = tbuf.at[k, :, pl.ds(32 * m, 32), :]
-            remote(dst, dst, t_send.at[0, 0], t_recv.at[k, m], a_target).wait_recv()
+    for p in range(PHASES):
+        if START[p] + 5 > last:
+            each(p, second)
+
+    remote(tbuf, tbuf, t_send.at[0, 0], t_recv, a_target).wait_recv()
     scale = 2.0 / math.sqrt(accounts)
     for j in range(2):
-        sums_out[j] = jnp.zeros((1, 128), jnp.float32)
+        for i in range(4):
+            back = tbuf[i // 2, i % 2, pl.ds(128 * j, 128), :].astype(jnp.float32).T
+            edge_ref[pl.ds(128 * i, 128), pl.ds(128 * j, 128)] = back * scale
+    for j in range(2):
+        column = jnp.zeros((1, 128), jnp.float32)
         for i in range(4):
             landed(1, i, j).wait_recv()
             landed(2, i, j).wait_recv()
             paths = part[s, h, i, j] + inbox[1, i, j] + inbox[2, i, j]
-            back = tbuf[i // 2, i % 2, pl.ds(128 * j, 128), :].astype(jnp.float32).T
-            value = paths * back * scale
-            edge_ref[pl.ds(128 * i, 128), pl.ds(128 * j, 128)] = value
-            sums_out[j] += jnp.sum(value, axis=0, keepdims=True)
-
-    def deliver(t):
-        cc = 16 * c + t
-        own = (y == z) & (h == s) & (cc == col)
-        copy = remote(
-            sums_out.at[t // 8], sums_in.at[row], s_send.at[t], s_recv.at[row], (2 * y + h, cc)
-        )
-        local = pltpu.make_async_copy(sums_out.at[t // 8], sums_in.at[row], s_recv.at[row])
-        return own, copy, local
-
-    for t in range(16):
-        own, copy, local = deliver(t)
-
-        @pl.when(own)
+            here = pl.ds(128 * i, 128), pl.ds(128 * j, 128)
+            value = paths * edge_ref[here]
+            edge_ref[here] = value
+            column += jnp.sum(value, axis=0, keepdims=True)
+        sums_out[j] = column
+
+    def deliver(t, which):
+        return remote(
+            sums_out.at[t // 8], sums_in.at[row], s_send.at[which], s_recv, (2 * y + h, 16 * c + t)
+        )
+
+    near = col % 16
+    own = (y == z) & (h == s) & (16 * c + near == col)
+    for q in range(15):
+        deliver((col + 1 + q) % 16, 0).start()
+
+    @pl.when(own)
+    def _():
+        pltpu.make_async_copy(sums_out.at[near // 8], sums_in.at[row], s_recv).start()
+
+    @pl.when(jnp.logical_not(own))
+    def _():
+        deliver(near, 1).start()
+
+    def left(ref, send):
+        remote(ref, ref, send, d_recv.at[0], a_target).wait_send()
+
+    @pl.when(jnp.logical_not(a_self))
+    def _():
+        left(w_ref, ra_send)
+
+    for half in range(2):
+        @pl.when(x != 2 * s + half)
         def _():
-            local.start()
-
-        @pl.when(jnp.logical_not(own))
-        def _():
-            copy.start()
-
-    for p in range(PHASES):
-        @pl.when(jnp.logical_not(a_self))
-        def _():
-            move_a(p).wait_send()
-
-        @pl.when((p + c) % 2 == h)
-        def _():
-            for half in range(2):
-                @pl.when(x != 2 * s + half)
-                def _():
-                    move_b(half, p // 2).wait_send()
-
-        for direction in (1, -1):
-            for k in range(steps(p, direction)):
-                hop_a(p, direction, k).wait_send()
-                hop_b(p, direction, k).wait_send()
-        for yy in range(8):
-            share(p, yy).wait_send()
-
-        @pl.loop(0, PHASES)
-        def _(i):
-            for k in range(2):
-                far, passes, direct, copy = roles(i, p, k)
-
-                @pl.when(far | passes | direct)
-                def _():
-                    copy.wait_send()
-
-    @pl.loop(0, 8)
-    def _(u):
+            left(w_ref.at[pl.ds(0, 256), :], rb_send.at[half])
+
+    left(a_buf.at[0, :, :, pl.ds(0, 1792)], y_send)
+    left(b_buf.at[:, :, pl.ds(0, 1792), :], z_send)
+    left(a_buf.at[0], d_send)
+    left(inbox, c_send)
+    for q in range(2):
         for hh in range(2):
-            own, copy, _ = mirror(u, hh)
-
-            @pl.when(jnp.logical_not(own))
+            mine, copy, _ = mirror(q, hh)
+
+            @pl.when(jnp.logical_not(mine))
             def _():
                 copy.wait_send()
 
-    total = jnp.zeros((1, 128), jnp.float32)
-    for r in range(16):
-        remote(sums_in.at[r], sums_in.at[r], s_send.at[r], s_recv.at[r], a_target).wait_recv()
-        total = total + sums_in[r]
-    total = total * (1.0 / math.sqrt(accounts))
-    share_of = pltpu.roll(total, lax.rem(128 - 16 * (col % 8), 128), 1)
-    acct_ref[...] = share_of[:, :16]
-    for t in range(16):
-        own, copy, _ = deliver(t)
-
-        @pl.when(jnp.logical_not(own))
-        def _():
-            copy.wait_send()
+    remote(sums_in, sums_in, s_send.at[0], s_recv, a_target).wait_recv()
+    total = jnp.sum(sums_in[...], axis=0) * (1.0 / math.sqrt(accounts))
+    acct_ref[...] = pltpu.roll(total, lax.rem(128 - 16 * (col % 8), 128), 1)[:, :16]
+    left(sums_in.at[pl.ds(0, 15)], s_send.at[0])
+
+    @pl.when(jnp.logical_not(own))
+    def _():
+        left(sums_in.at[pl.ds(0, 1)], s_send.at[1])
 
 
 def body(weights):
@@ -370,9 +361,9 @@
             pltpu.VMEM((2, 2, 256, 128), jnp.bfloat16),
             pltpu.VMEM((2, 1, 128), jnp.float32),
             pltpu.VMEM((16, 1, 128), jnp.float32),
-            dma((4,)), dma((4,)), dma((2, 2)), dma((2, 2)),
-            dma((4, 2, 4)), dma((4, 8)), dma((4, 2, 4)), dma((4, 8)), dma((4, 8)), dma((4, 8)),
-            dma((2, 2, 4, 2)), dma((3, 4, 2)), dma((8, 2)), dma((2, 8)), dma((16,)), dma((16,)),
+            dma, dma((4,)), dma((2,)), dma((2, 2)),
+            dma, dma((4, 8)), dma, dma((4, 8)), dma, dma((4,)),
+            dma, dma((3, 4, 2)), dma((2, 2)), dma, dma((2,)), dma,
         ],
         compiler_params=pltpu.CompilerParams(
             collective_id=0, has_side_effects=True, vmem_limit_bytes=32 * 1024 * 1024

time: 90.2 us -> 76.2 us (0.84)
  the two profiles are of different devices: /device:TPU:2 before, /device:TPU:450 now
where the time goes in v2:
time: 76.2 us; the launch traced here: 76.1 us
  Pallas kernels  73.2 us (96%)
  local copies, waits for them, and re-layouts  2.25 us (3%)
    pallas_call x1, Pallas kernels, body(): pl.pallas_call(kernel, out_shape=(jax.ShapeDtypeStruct((512, 256), jnp.fl...  73.2 us
    unnamed x4, local copies, waits for them, and re-layouts  2.25 us

profile of v2, /device:TPU:450, one launch (start us, length us, event | category | flops | bytes accessed | tf_op | source)
XLA Modules:
  0.0 76.1 jit_solution(13256658457391095970)
XLA Ops:
  0.6 0.0 copy-start
  0.6 0.9 %copy-done = bf16[512,256]{1,0:T(8,128)(2,1)S(1)} copy-done((bf16[512,256]{1,0:T(8,128)(2,1)S(1)}, bf16[512,256]{1,0:T(8,128)(2,1)}, u32[]{:S(2)}) %copy-start) | copy-done | bytes 262168
  1.6 73.2 %cycles.1 = (f32[512,256]{1,0:T(8,128)S(1)}, f32[1,16]{1,0:T(1,128)S(1)}) custom-call(bf16[512,256]{1,0:T(8,128)(2,1)S(1)} %copy-done), custom_call_target="tpu_custom_call" | custom-call | tf_op jit(solution)/shard_map/cycles/pallas_call | solution.py:345
  74.8 0.8 %copy.5 = f32[512,256]{1,0:T(8,128)} copy(f32[512,256]{1,0:T(8,128)S(1)} %get-tuple-element.8) | data formatting | bytes 1048576
  75.5 0.5 copy.6
Async XLA Ops:
  0.6 1.0 %copy-start = (bf16[512,256]{1,0:T(8,128)(2,1)S(1)}, bf16[512,256]{1,0:T(8,128)(2,1)}, u32[]{:S(2)}) copy-start(bf16[512,256]{1,0:T(8,128)(2,1)} %w_ref.1) | copy-start | bytes 786436

commit v3 on v2

v3 whole, which is shorter than its diff:
```python
import math

import jax
import jax.numpy as jnp
from jax import lax
from jax.experimental import pallas as pl
from jax.experimental.pallas import tpu as pltpu
from jax.sharding import PartitionSpec as P

MESH = pl.DeviceIdType.MESH
PHASES = 4
SUBS = 2 * PHASES
START = (0,) * SUBS


def kernel(
    w_ref, edge_ref, acct_ref,
    a_buf, b_buf, part, inbox, tbuf, sums_out, sums_in,
    ra_send, ra_recv, rb_send, rb_recv,
    y_send, y_recv, z_send, z_recv, d_send, d_recv,
    c_send, c_recv, t_send, t_recv, s_send, s_recv, ready,
):
    row, col = lax.axis_index("row"), lax.axis_index("col")
    z, s = row // 2, row % 2
    y, h, c = col // 4, (col // 2) % 2, col % 2
    x = 2 * h + s
    accounts = 8192

    def dev(y_, z_, x_, c_):
        return (2 * z_ + x_ % 2, 4 * y_ + 2 * (x_ // 2) + c_)

    def up(v, d, n):
        return lax.rem(v + (d + n), n)

    def remote(src, dst, send, recv, target):
        return pltpu.make_async_remote_copy(
            src_ref=src, dst_ref=dst, send_sem=send, recv_sem=recv,
            device_id=target, device_id_type=MESH,
        )

    barrier = pltpu.get_barrier_semaphore()
    senders = [
        dev(up(y, 1, 8), z, x, c), dev(up(y, -1, 8), z, x, c),
        dev(y, up(z, 1, 8), x, c), dev(y, up(z, -1, 8), x, c),
        dev(y, z, x, 1 - c),
    ]
    for step in range(1, 4):
        for k in range(2):
            senders.append(dev(y, z, up(x, step, 4), k))
    for target in senders:
        pl.semaphore_signal(barrier, inc=1, device_id=target, device_id_type=MESH)
    pl.semaphore_wait(barrier, len(senders))

    a_self = s == c
    a_target = dev(y, z, 2 * h + c, s)

    def lanes(v):
        return pl.ds(pl.multiple_of(v * 256, 256), 256)

    def rows(v, q):
        return pl.ds(pl.multiple_of(v * 256 + 128 * (q % 2), 128), 128)

    def a_block(owner, q, yy):
        return a_buf.at[owner, q // 2, pl.ds(64 * (q % 2), 64), lanes(yy)]

    def b_block(q, zz):
        p = q // 2
        return b_buf.at[(p + c) % 2, p // 2, rows(zz, q), :]

    def move_a(q):
        return w_ref.at[pl.ds(64 * q, 64), :], a_block(s, q, y), ra_recv.at[q]

    def move_b(half, q):
        src = w_ref.at[pl.ds(256 * half + 128 * (q % 2), 128), pl.ds(128 * (q // 4), 128)]
        return src, b_block(q, z), rb_recv.at[q]

    for q in range(SUBS):
        src, dst, arrived = move_a(q)

        @pl.when(a_self)
        def _():
            pltpu.make_async_copy(src, dst, arrived).start()

        @pl.when(jnp.logical_not(a_self))
        def _():
            remote(src, dst, ra_send, arrived, a_target).start()

        @pl.when((q // 2 + c) % 2 == h)
        def _():
            for half in range(2):
                src, dst, arrived = move_b(half, q)

                @pl.when(x == 2 * s + half)
                def _():
                    pltpu.make_async_copy(src, dst, arrived).start()

                @pl.when(x != 2 * s + half)
                def _():
                    remote(src, dst, rb_send.at[half], arrived, dev(y, z, 2 * s + half, c)).start()

    def hop_a(q, direction, k):
        yy = up(y, -direction * k, 8)
        block = a_block(c, q, yy)
        return remote(block, block, y_send, y_recv.at[q, yy], dev(up(y, direction, 8), z, x, c))

    def hop_b(q, direction, k):
        zz = up(z, -direction * k, 8)
        block = b_block(q, zz)
        return remote(block, block, z_send, z_recv.at[q, zz], dev(y, up(z, direction, 8), x, c))

    def share(q, yy):
        block = a_block(c, q, yy)
        return remote(block, block, d_send, d_recv.at[q // 2], dev(y, z, x, 1 - c))

    def shared(p):
        block = a_buf.at[1 - c, p]
        return remote(block, block, d_send, d_recv.at[p], a_target)

    def steps(q, direction):
        return 3 + (q + (1 + direction) // 2) % 2

    def place(i, p):
        return (p + c) % 2, p // 2, 1 - 2 * ((i + p // 2) % 2)

    def product(i, p):
        hh, j, _ = place(i, p)
        left = a_buf[:, i].reshape(256, 2048)
        value = jnp.dot(left, b_buf[hh, j], preferred_element_type=jnp.float32)
        part[0, hh, i, j] = value[:128]
        part[1, hh, i, j] = value[128:]

    def roles(i, p, k):
        hh, j, way = place(i, p)
        delta = lax.rem(2 * hh + k + 4 - x, 4)
        relay = lax.rem(way + 4, 4)
        far = delta == 2
        passes = delta == relay
        direct = jnp.logical_and(delta % 2 == 1, jnp.logical_not(passes))
        step = jnp.where(far, way, 2 - delta)
        kind = jnp.where(far, 0, (delta + 1) // 2)
        copy = remote(
            part.at[k, hh, i, j], inbox.at[kind, i, j], c_send, c_recv.at[kind, i, j],
            dev(y, z, lax.rem(x + step + 4, 4), c),
        )
        return far, passes, direct, copy

    def landed(kind, i, j):
        return remote(
            inbox.at[kind, i, j], inbox.at[kind, i, j], c_send, c_recv.at[kind, i, j],
            a_target,
        )

    def tiles(q):
        return [(q, p) for p in range(q + 1)], [(i, q) for i in range(q)]

    def each(q, action):
        @pl.loop(0, q + 1)
        def _(p):
            action(q, p)

        if q:
            @pl.loop(0, q)
            def _(i):
                action(i, q)

    def first(i, p):
        product(i, p)
        for k in range(2):
            far, _, direct, copy = roles(i, p, k)

            @pl.when(jnp.logical_or(far, direct))
            def _():
                copy.start()

    def second(i, p):
        hh, j, _ = place(i, p)
        for k in range(2):
            _, passes, _, copy = roles(i, p, k)

            @pl.when(passes)
            def _():
                landed(0, i, j).wait_recv()
                part[k, hh, i, j] += inbox[0, i, j]
                copy.start()

    def mirror(q, hh):
        u = (z + 8 - y) % 4 + 4 * q
        half = z // 4
        src = b_buf.at[hh, :, pl.ds(pl.multiple_of(u * 256 + half * 128, 128), 128), :]
        dst = tbuf.at[c, :, pl.ds(pl.multiple_of(half * 128, 128), 128), :]
        own = (u == y) & (hh == s) & (s == c) & (y == z)
        copy = remote(src, dst, t_send.at[q, hh], t_recv, dev(u, y, 2 * h + hh, s))
        local = pltpu.make_async_copy(src, dst, t_recv)
        return own, copy, local

    ends = [max(START[2 * p], START[2 * p + 1]) + 4 for p in range(PHASES)]
    last = max(ends)
    for slot in range(last + 1):
        for q in range(SUBS):
            k = slot - START[q]
            if k == 0:
                block = a_block(c, q, y)
                remote(block, block, ra_send, ra_recv.at[q], a_target).wait_recv()
                for direction in (1, -1):
                    hop_a(q, direction, 0).start()
                block = b_block(q, z)
                remote(block, block, ra_send, rb_recv.at[q], a_target).wait_recv()
                for direction in (1, -1):
                    hop_b(q, direction, 0).start()
                share(q, y).start()
            elif 1 <= k <= 4:
                for direction in (1, -1):
                    if k <= steps(q, direction):
                        hop_a(q, direction, k).wait_recv()
                        if k < steps(q, direction):
                            hop_a(q, direction, k).start()
                        hop_b(q, direction, k).wait_recv()
                        if k < steps(q, direction):
                            hop_b(q, direction, k).start()
                        share(q, up(y, -direction * k, 8)).start()
        if slot == START[0] + 4:
            for k in range(1, 8):
                pl.semaphore_signal(
                    ready, inc=1, device_id=dev(up(y, k, 8), z, x, c), device_id_type=MESH
                )
        for p in range(PHASES):
            if slot == ends[p]:
                shared(p).wait_recv()
                each(p, first)
            elif slot == ends[p] + 1:
                each(p, second)
    pl.semaphore_wait(ready, 7)
    for q in range(2):
        for hh in range(2):
            mine, copy, local = mirror(q, hh)

            @pl.when(mine)
            def _():
                local.start()

            @pl.when(jnp.logical_not(mine))
            def _():
                copy.start()

    for p in range(PHASES):
        if ends[p] == last:
            each(p, second)

    remote(tbuf, tbuf, t_send.at[0, 0], t_recv, a_target).wait_recv()
    scale = 2.0 / math.sqrt(accounts)
    for j in range(2):
        for i in range(4):
            back = tbuf[i // 2, i % 2, pl.ds(128 * j, 128), :].astype(jnp.float32).T
            edge_ref[pl.ds(128 * i, 128), pl.ds(128 * j, 128)] = back * scale
    for i in range(4):
        both = jnp.zeros((128, 128), jnp.float32)
        for j in range(2):
            landed(1, i, j).wait_recv()
            landed(2, i, j).wait_recv()
            paths = part[s, h, i, j] + inbox[1, i, j] + inbox[2, i, j]
            here = pl.ds(128 * i, 128), pl.ds(128 * j, 128)
            value = paths * edge_ref[here]
            edge_ref[here] = value
            both += value
        sums_out[i] = jnp.sum(both.T, axis=0, keepdims=True)

    for q in range(31):
        t = (col + 1 + q) % 32
        remote(sums_out.at[t // 8], sums_in.at[col], s_send, s_recv, (row, t)).start()
    sums_in[col] = sums_out[col // 8]

    def left(ref, send):
        remote(ref, ref, send, d_recv.at[0], a_target).wait_send()

    @pl.when(jnp.logical_not(a_self))
    def _():
        left(w_ref, ra_send)

    for half in range(2):
        @pl.when(x != 2 * s + half)
        def _():
            left(w_ref.at[pl.ds(0, 256), :], rb_send.at[half])

    left(a_buf.at[0, :, :, pl.ds(0, 1792)], y_send)
    left(b_buf.at[:, :, pl.ds(0, 1792), :], z_send)
    left(a_buf.at[0], d_send)
    left(inbox, c_send)
    for q in range(2):
        for hh in range(2):
            mine, copy, _ = mirror(q, hh)

            @pl.when(jnp.logical_not(mine))
            def _():
                copy.wait_send()

    others = sums_in.at[pl.ds(0, 31)]
    remote(others, others, s_send, s_recv, a_target).wait_recv()
    total = jnp.sum(sums_in[...], axis=0) * (1.0 / math.sqrt(accounts))
    acct_ref[...] = pltpu.roll(total, lax.rem(128 - 16 * (col % 8), 128), 1)[:, :16]
    left(others, s_send)


def body(weights):
    dma = pltpu.SemaphoreType.DMA
    edge, acct = pl.pallas_call(
        kernel,
        out_shape=(
            jax.ShapeDtypeStruct((512, 256), jnp.float32),
            jax.ShapeDtypeStruct((1, 16), jnp.float32),
        ),
        in_specs=[pl.BlockSpec(memory_space=pltpu.VMEM)],
        out_specs=(
            pl.BlockSpec(memory_space=pltpu.VMEM),
            pl.BlockSpec(memory_space=pltpu.VMEM),
        ),
        scratch_shapes=[
            pltpu.VMEM((2, 4, 128, 2048), jnp.bfloat16),
            pltpu.VMEM((2, 2, 2048, 128), jnp.bfloat16),
            pltpu.VMEM((2, 2, 4, 2, 128, 128), jnp.float32),
            pltpu.VMEM((3, 4, 2, 128, 128), jnp.float32),
            pltpu.VMEM((2, 2, 256, 128), jnp.bfloat16),
            pltpu.VMEM((4, 1, 128), jnp.float32),
            pltpu.VMEM((32, 1, 128), jnp.float32),
            dma, dma((8,)), dma((2,)), dma((8,)),
            dma, dma((8, 8)), dma, dma((8, 8)), dma, dma((4,)),
            dma, dma((3, 4, 2)), dma((2, 2)), dma, dma, dma, pltpu.SemaphoreType.REGULAR,
        ],
        compiler_params=pltpu.CompilerParams(
            collective_id=0, has_side_effects=True, vmem_limit_bytes=32 * 1024 * 1024
        ),
        name="cycles",
    )(weights)
    return edge, acct.reshape(16)


def solution(mesh):
    return jax.shard_map(
        body,
        mesh=mesh,
        in_specs=(P("row", "col"),),
        out_specs=(P("row", "col"), P(("row", "col"))),
        check_vma=False,
    )
```

time: 76.2 us -> 73.4 us (0.963)
  the two profiles are of different devices: /device:TPU:450 before, /device:TPU:1 now
where the time goes in v3:
time: 73.4 us; the launch traced here: 73.3 us
  Pallas kernels  70.4 us (96%)
  local copies, waits for them, and re-layouts  2.25 us (3%)
    pallas_call x1, Pallas kernels, body(): pl.pallas_call(kernel, out_shape=(jax.ShapeDtypeStruct((512, 256), jnp.fl...  70.4 us
    unnamed x4, local copies, waits for them, and re-layouts  2.25 us

profile of v3, /device:TPU:1, one launch (start us, length us, event | category | flops | bytes accessed | tf_op | source)
XLA Modules:
  0.0 73.3 jit_solution(11281388966703229202)
XLA Ops:
  0.6 0.0 copy-start
  0.6 0.9 %copy-done = bf16[512,256]{1,0:T(8,128)(2,1)S(1)} copy-done((bf16[512,256]{1,0:T(8,128)(2,1)S(1)}, bf16[512,256]{1,0:T(8,128)(2,1)}, u32[]{:S(2)}) %copy-start) | copy-done | bytes 262168
  1.6 70.4 %cycles.1 = (f32[512,256]{1,0:T(8,128)S(1)}, f32[1,16]{1,0:T(1,128)S(1)}) custom-call(bf16[512,256]{1,0:T(8,128)(2,1)S(1)} %copy-done), custom_call_target="tpu_custom_call" | custom-call | tf_op jit(solution)/shard_map/cycles/pallas_call | solution.py:305
  72.0 0.8 %copy.5 = f32[512,256]{1,0:T(8,128)} copy(f32[512,256]{1,0:T(8,128)S(1)} %get-tuple-element.8) | data formatting | bytes 1048576
  72.8 0.5 copy.6
Async XLA Ops:
  0.6 1.0 %copy-start = (bf16[512,256]{1,0:T(8,128)(2,1)S(1)}, bf16[512,256]{1,0:T(8,128)(2,1)}, u32[]{:S(2)}) copy-start(bf16[512,256]{1,0:T(8,128)(2,1)} %w_ref.1) | copy-start | bytes 786436

commit v4 on v3

--- a/solution.py
+++ b/solution.py
@@ -10,7 +10,7 @@
 MESH = pl.DeviceIdType.MESH
 PHASES = 4
 SUBS = 2 * PHASES
-START = (0,) * SUBS
+STEPS = 4
 
 
 def kernel(
@@ -119,22 +119,18 @@
     def steps(q, direction):
         return 3 + (q + (1 + direction) // 2) % 2
 
-    def place(i, p):
-        return (p + c) % 2, p // 2, 1 - 2 * ((i + p // 2) % 2)
-
-    def product(i, p):
-        hh, j, _ = place(i, p)
+    def product(i, hh):
         left = a_buf[:, i].reshape(256, 2048)
-        value = jnp.dot(left, b_buf[hh, j], preferred_element_type=jnp.float32)
-        part[0, hh, i, j] = value[:128]
-        part[1, hh, i, j] = value[128:]
-
-    def roles(i, p, k):
-        hh, j, way = place(i, p)
+        right = jnp.concatenate([b_buf[hh, 0], b_buf[hh, 1]], axis=1)
+        value = jnp.dot(left, right, preferred_element_type=jnp.float32)
+        for k in range(2):
+            for j in range(2):
+                part[k, hh, i, j] = value[128 * k : 128 * k + 128, 128 * j : 128 * j + 128]
+
+    def roles(i, hh, j, k):
+        way = 1 - 2 * ((i + j) % 2)
         delta = lax.rem(2 * hh + k + 4 - x, 4)
-        relay = lax.rem(way + 4, 4)
-        far = delta == 2
-        passes = delta == relay
+        far, passes = delta == 2, delta == lax.rem(way + 4, 4)
         direct = jnp.logical_and(delta % 2 == 1, jnp.logical_not(passes))
         step = jnp.where(far, way, 2 - delta)
         kind = jnp.where(far, 0, (delta + 1) // 2)
@@ -145,43 +141,26 @@
         return far, passes, direct, copy
 
     def landed(kind, i, j):
-        return remote(
-            inbox.at[kind, i, j], inbox.at[kind, i, j], c_send, c_recv.at[kind, i, j],
-            a_target,
-        )
-
-    def tiles(q):
-        return [(q, p) for p in range(q + 1)], [(i, q) for i in range(q)]
-
-    def each(q, action):
-        @pl.loop(0, q + 1)
-        def _(p):
-            action(q, p)
-
-        if q:
-            @pl.loop(0, q)
-            def _(i):
-                action(i, q)
-
-    def first(i, p):
-        product(i, p)
-        for k in range(2):
-            far, _, direct, copy = roles(i, p, k)
-
-            @pl.when(jnp.logical_or(far, direct))
-            def _():
-                copy.start()
-
-    def second(i, p):
-        hh, j, _ = place(i, p)
-        for k in range(2):
-            _, passes, _, copy = roles(i, p, k)
-
-            @pl.when(passes)
-            def _():
-                landed(0, i, j).wait_recv()
-                part[k, hh, i, j] += inbox[0, i, j]
-                copy.start()
+        block = inbox.at[kind, i, j]
+        return remote(block, block, c_send, c_recv.at[kind, i, j], a_target)
+
+    def first(i, hh):
+        product(i, hh)
+        for j in range(2):
+            for k in range(2):
+                far, _, direct, copy = roles(i, hh, j, k)
+                pl.when(jnp.logical_or(far, direct))(copy.start)
+
+    def second(i, hh):
+        for j in range(2):
+            for k in range(2):
+                _, passes, _, copy = roles(i, hh, j, k)
+
+                @pl.when(passes)
+                def _():
+                    landed(0, i, j).wait_recv()
+                    part[k, hh, i, j] += inbox[0, i, j]
+                    copy.start()
 
     def mirror(q, hh):
         u = (z + 8 - y) % 4 + 4 * q
@@ -193,58 +172,49 @@
         local = pltpu.make_async_copy(src, dst, t_recv)
         return own, copy, local
 
-    ends = [max(START[2 * p], START[2 * p + 1]) + 4 for p in range(PHASES)]
-    last = max(ends)
-    for slot in range(last + 1):
+    for q in range(SUBS):
+        block = a_block(c, q, y)
+        remote(block, block, ra_send, ra_recv.at[q], a_target).wait_recv()
+        for direction in (1, -1):
+            hop_a(q, direction, 0).start()
+        block = b_block(q, z)
+        remote(block, block, ra_send, rb_recv.at[q], a_target).wait_recv()
+        for direction in (1, -1):
+            hop_b(q, direction, 0).start()
+        share(q, y).start()
+    for k in range(1, STEPS + 1):
         for q in range(SUBS):
-            k = slot - START[q]
-            if k == 0:
-                block = a_block(c, q, y)
-                remote(block, block, ra_send, ra_recv.at[q], a_target).wait_recv()
-                for direction in (1, -1):
-                    hop_a(q, direction, 0).start()
-                block = b_block(q, z)
-                remote(block, block, ra_send, rb_recv.at[q], a_target).wait_recv()
-                for direction in (1, -1):
-                    hop_b(q, direction, 0).start()
-                share(q, y).start()
-            elif 1 <= k <= 4:
-                for direction in (1, -1):
-                    if k <= steps(q, direction):
-                        hop_a(q, direction, k).wait_recv()
-                        if k < steps(q, direction):
-                            hop_a(q, direction, k).start()
-                        hop_b(q, direction, k).wait_recv()
-                        if k < steps(q, direction):
-                            hop_b(q, direction, k).start()
-                        share(q, up(y, -direction * k, 8)).start()
-        if slot == START[0] + 4:
-            for k in range(1, 8):
-                pl.semaphore_signal(
-                    ready, inc=1, device_id=dev(up(y, k, 8), z, x, c), device_id_type=MESH
-                )
-        for p in range(PHASES):
-            if slot == ends[p]:
-                shared(p).wait_recv()
-                each(p, first)
-            elif slot == ends[p] + 1:
-                each(p, second)
+            for direction in (1, -1):
+                if k <= steps(q, direction):
+                    hop_a(q, direction, k).wait_recv()
+                    if k < steps(q, direction):
+                        hop_a(q, direction, k).start()
+                    share(q, up(y, -direction * k, 8)).start()
+                    hop_b(q, direction, k).wait_recv()
+                    if k < steps(q, direction):
+                        hop_b(q, direction, k).start()
+    for k in range(1, 8):
+        pl.semaphore_signal(
+            ready, inc=1, device_id=dev(up(y, k, 8), z, x, c), device_id_type=MESH
+        )
+
+    @pl.loop(0, PHASES)
+    def _(i):
+        shared(i).wait_recv()
+        first(i, 0)
+        first(i, 1)
+
     pl.semaphore_wait(ready, 7)
     for q in range(2):
         for hh in range(2):
             mine, copy, local = mirror(q, hh)
-
-            @pl.when(mine)
-            def _():
-                local.start()
-
-            @pl.when(jnp.logical_not(mine))
-            def _():
-                copy.start()
-
-    for p in range(PHASES):
-        if ends[p] == last:
-            each(p, second)
+            pl.when(mine)(local.start)
+            pl.when(jnp.logical_not(mine))(copy.start)
+
+    @pl.loop(0, PHASES)
+    def _(i):
+        second(i, 0)
+        second(i, 1)
 
     remote(tbuf, tbuf, t_send.at[0, 0], t_recv, a_target).wait_recv()
     scale = 2.0 / math.sqrt(accounts)
@@ -263,10 +233,13 @@
             edge_ref[here] = value
             both += value
         sums_out[i] = jnp.sum(both.T, axis=0, keepdims=True)
-
-    for q in range(31):
-        t = (col + 1 + q) % 32
-        remote(sums_out.at[t // 8], sums_in.at[col], s_send, s_recv, (row, t)).start()
+        for k in range(1, 9):
+            t = 8 * i + (col + k) % 8
+            copy = remote(sums_out.at[i], sums_in.at[col], s_send, s_recv, (row, t))
+            if k < 8:
+                copy.start()
+            else:
+                pl.when(t != col)(copy.start)
     sums_in[col] = sums_out[col // 8]
 
     def left(ref, send):

time: 73.4 us -> 70.9 us (0.966)
  Pallas kernels: 70.4 us -> 67.3 us
    pallas_call x1, Pallas kernels: 70.4 us -> 67.3 us  [body(): pl.pallas_call(kernel, out_shape=(jax.ShapeDtypeStruct((512, 256), jnp.fl...]
where the time goes in v4:
time: 70.9 us; the launch traced here: 70.2 us
  Pallas kernels  67.3 us (95%)
  local copies, waits for them, and re-layouts  2.25 us (3%)
    pallas_call x1, Pallas kernels, body(): pl.pallas_call(kernel, out_shape=(jax.ShapeDtypeStruct((512, 256), jnp.fl...  67.3 us
    unnamed x4, local copies, waits for them, and re-layouts  2.25 us

profile of v4, /device:TPU:1, one launch (start us, length us, event | category | flops | bytes accessed | tf_op | source)
XLA Modules:
  0.0 70.2 jit_solution(15907268115236686929)
XLA Ops:
  0.6 0.0 copy-start
  0.6 0.9 %copy-done = bf16[512,256]{1,0:T(8,128)(2,1)S(1)} copy-done((bf16[512,256]{1,0:T(8,128)(2,1)S(1)}, bf16[512,256]{1,0:T(8,128)(2,1)}, u32[]{:S(2)}) %copy-start) | copy-done | bytes 262168
  1.6 67.3 %cycles.1 = (f32[512,256]{1,0:T(8,128)S(1)}, f32[1,16]{1,0:T(1,128)S(1)}) custom-call(bf16[512,256]{1,0:T(8,128)(2,1)S(1)} %copy-done), custom_call_target="tpu_custom_call" | custom-call | tf_op jit(solution)/shard_map/cycles/pallas_call | solution.py:278
  68.9 0.8 %copy.5 = f32[512,256]{1,0:T(8,128)} copy(f32[512,256]{1,0:T(8,128)S(1)} %get-tuple-element.8) | data formatting | bytes 1048576
  69.7 0.5 copy.6
Async XLA Ops:
  0.6 1.0 %copy-start = (bf16[512,256]{1,0:T(8,128)(2,1)S(1)}, bf16[512,256]{1,0:T(8,128)(2,1)}, u32[]{:S(2)}) copy-start(bf16[512,256]{1,0:T(8,128)(2,1)} %w_ref.1) | copy-start | bytes 786436

commit v5 on v4

--- a/solution.py
+++ b/solution.py
@@ -146,10 +146,11 @@
 
     def first(i, hh):
         product(i, hh)
-        for j in range(2):
-            for k in range(2):
-                far, _, direct, copy = roles(i, hh, j, k)
-                pl.when(jnp.logical_or(far, direct))(copy.start)
+        for turn in (0, 2):
+            for j in range(2):
+                for k in range(2):
+                    copies = roles(i, hh, j, k)
+                    pl.when(copies[turn])(copies[3].start)
 
     def second(i, hh):
         for j in range(2):

time: 70.9 us -> 71 us (level)
  no operation moved by 1% of the time
where the time goes in v5:
time: 71 us; the launch traced here: 70.1 us
  Pallas kernels  67.2 us (95%)
  local copies, waits for them, and re-layouts  2.25 us (3%)
    pallas_call x1, Pallas kernels, body(): pl.pallas_call(kernel, out_shape=(jax.ShapeDtypeStruct((512, 256), jnp.fl...  67.2 us
    unnamed x4, local copies, waits for them, and re-layouts  2.25 us

profile of v5, /device:TPU:1, one launch (start us, length us, event | category | flops | bytes accessed | tf_op | source)
XLA Modules:
  0.0 70.1 jit_solution(13440282785036518271)
XLA Ops:
  0.6 0.0 copy-start
  0.6 0.9 %copy-done = bf16[512,256]{1,0:T(8,128)(2,1)S(1)} copy-done((bf16[512,256]{1,0:T(8,128)(2,1)S(1)}, bf16[512,256]{1,0:T(8,128)(2,1)}, u32[]{:S(2)}) %copy-start) | copy-done | bytes 262168
  1.6 67.2 %cycles.1 = (f32[512,256]{1,0:T(8,128)S(1)}, f32[1,16]{1,0:T(1,128)S(1)}) custom-call(bf16[512,256]{1,0:T(8,128)(2,1)S(1)} %copy-done), custom_call_target="tpu_custom_call" | custom-call | tf_op jit(solution)/shard_map/cycles/pallas_call | solution.py:279
  68.8 0.8 %copy.5 = f32[512,256]{1,0:T(8,128)} copy(f32[512,256]{1,0:T(8,128)S(1)} %get-tuple-element.8) | data formatting | bytes 1048576
  69.6 0.5 copy.6
Async XLA Ops:
  0.6 1.0 %copy-start = (bf16[512,256]{1,0:T(8,128)(2,1)S(1)}, bf16[512,256]{1,0:T(8,128)(2,1)}, u32[]{:S(2)}) copy-start(bf16[512,256]{1,0:T(8,128)(2,1)} %w_ref.1) | copy-start | bytes 786436
